TPU v7x, 32 devices: a whole 2x2x4 slice. The times are simulated.
32 devices in a mesh: dp: 4 (over z), mp: 8 (over y, x, core).
Axes of the slice: x: 2, y: 2, z: 4, core: 2. Of those that a mesh axis runs over, the one named last changes fastest.
Arguments:
- activations: bfloat16 [8192, 8192], P('dp', 'mp'), as said below
- output_grads: bfloat16 [8192, 28672], P('dp', 'mp'), as said below
- probe_matrix: bfloat16 [28672, 128], P('mp'), may hold values from -6 to 6
Outputs:
- basis: float32 [8192, 128], P('mp')
- projection: float32 [128, 28672], P(None, 'mp')
Inputs may be any that keep to these rules, and one draw needn't show every extreme that they name: `activations`: finite real values of order one. `output_grads`: finite real values of order one.
All inputs are finite; a program needn't handle non-finite values.
Results may differ from a plain program's by a relative error of at most 0.035.
Values may be sent and summed in bfloat16 or wider, within the bound.
A program may use at most 64 MiB of HBM per device.

v0:
```python
import jax
import jax.numpy as jnp
from jax import lax
from jax.sharding import PartitionSpec as P

H = 8192


def contract_rows(left, right):
    return lax.dot_general(
        left, right, (((0,), (0,)), ((), ())), preferred_element_type=jnp.float32
    )


def token_total(partial_value):
    return lax.psum(partial_value.astype(jnp.bfloat16), "mp")


def gram_of(matrix):
    return lax.dot_general(
        matrix,
        matrix,
        (((0,), (0,)), ((), ())),
        precision=lax.Precision.HIGHEST,
        preferred_element_type=jnp.float32,
    )


def solve_rows(factor, matrix):
    return lax.linalg.triangular_solve(
        factor, matrix, left_side=False, lower=True, transpose_a=True
    )


def orthonormalize(partial_value):
    summed = lax.psum(partial_value, "dp")
    gram_matrix = lax.psum(gram_of(summed), "mp")
    factor = jnp.linalg.cholesky(gram_matrix)
    return solve_rows(factor, summed)


def on_device(activations, output_grads, probe_matrix):
    probe_rows = token_total(
        jnp.dot(output_grads, probe_matrix, preferred_element_type=jnp.float32)
    )
    first_basis = orthonormalize(contract_rows(activations, probe_rows))
    token_rows = token_total(
        jnp.dot(activations, first_basis.astype(jnp.bfloat16), preferred_element_type=jnp.float32)
    )
    second_basis = orthonormalize(contract_rows(output_grads, token_rows))
    unit_rows = token_total(
        jnp.dot(output_grads, second_basis.astype(jnp.bfloat16), preferred_element_type=jnp.float32)
    )
    third_basis = orthonormalize(contract_rows(activations, unit_rows))
    last_rows = token_total(
        jnp.dot(activations, third_basis.astype(jnp.bfloat16), preferred_element_type=jnp.float32)
    )
    projected = contract_rows(last_rows, output_grads)
    projection = lax.psum(projected, "dp")
    basis = third_basis * jnp.sqrt(jnp.float32(H))
    return (basis, projection)


def solution(mesh):
    in_specs = (P("dp", "mp"), P("dp", "mp"), P("mp", None))
    out_specs = (P("mp", None), P(None, "mp"))
    return jax.shard_map(
        on_device, mesh=mesh, in_specs=in_specs, out_specs=out_specs, check_vma=False
    )
```

profile of v0, /device:TPU:0, one launch (start us, length us, event | category | flops | bytes accessed | tf_op | source)
XLA Modules:
  0.0 770.1 jit_solution(543548165452098661)
XLA Ops:
  8.3 8.1 %convolution_convert_fusion.4 = bf16[2048,128]{1,0:T(8,128)(2,1)} fusion(bf16[2048,3584]{1,0:T(8,128)(2,1)} %param.7, bf16[3584,128]{1,0:T(8,128)(2,1)S(1)} %copy-done), kind=kOutput, calls=%fused_computation.5 | convolution fusion | flops 1879310336 | bytes 16121856 | tf_op jit(solution)/shard_map/dot_general | solution.py:44
  16.5 57.3 %all-reduce.12.cloned.1.call-done = bf16[2048,128]{1,0:T(8,128)(2,1)} async-done(((bf16[2048,128]{1,0:T(8,128)(2,1)}), bf16[2048,128]{1,0:T(8,128)(2,1)}) %all-reduce.12.cloned.1.call-update) | async-done | bytes 524304 | tf_op jit(solution)/shard_map/psum | solution.py:16
  77.8 37.7 %all-reduce.14.cloned.1.call-done = f32[1024,128]{0,1:T(8,128)} async-done(((f32[1024,128]{0,1:T(8,128)}), f32[1024,128]{0,1:T(8,128)}) %all-reduce.14.cloned.1.call-update) | async-done | bytes 524304 | tf_op jit(solution)/shard_map/psum | solution.py:36
  118.0 53.9 %all-reduce.16.cloned.1.call-done = f32[128,128]{0,1:T(8,128)} async-done(((f32[128,128]{0,1:T(8,128)}), f32[128,128]{0,1:T(8,128)}) %all-reduce.16.cloned.1.call-update) | async-done | bytes 65552 | tf_op jit(solution)/shard_map/psum | solution.py:37
  173.7 11.7 %cholesky.59 = f32[128,128]{1,0:T(8,128)S(1)} custom-call(f32[128,128]{1,0:T(8,128)S(1)} %fusion.13), custom_call_target="Cholesky" | custom-call | tf_op jit(solution)/shard_map/jit(cholesky)/cholesky | solution.py:38
  186.7 9.8 %custom-call.10 = f32[1,128,128]{1,2,0:T(8,128)S(1)} custom-call(f32[1,128,128]{2,1,0:T(8,128)S(1)} %fusion.5), custom_call_target="InvertDiagBlocksLowerTriangular" | custom-call | tf_op jit(solution)/shard_map/triangular_solve/custom-call.0 | solution.py:30
  198.2 4.5 fusion
  203.1 53.8 %all-reduce.18.cloned.1.call-done = bf16[2048,128]{0,1:T(8,128)(2,1)} async-done(((bf16[2048,128]{0,1:T(8,128)(2,1)}), bf16[2048,128]{0,1:T(8,128)(2,1)}) %all-reduce.18.cloned.1.call-update) | async-done | bytes 524304 | tf_op jit(solution)/shard_map/psum | solution.py:16
  256.9 8.7 %convolution_bitcast_fusion = f32[3584,128]{0,1:T(8,128)} fusion(bf16[2048,128]{0,1:T(8,128)(2,1)} %all-reduce.18.cloned.1.call-done, bf16[2048,3584]{1,0:T(8,128)(2,1)} %param.7), kind=kOutput, calls=%fused_computation | convolution fusion | flops 1879048192 | bytes 17039360 | tf_op jit(solution)/shard_map/dot_general | solution.py:10
  265.6 77.1 %all-reduce.20.cloned.1.call-done = f32[3584,128]{0,1:T(8,128)} async-done(((f32[3584,128]{0,1:T(8,128)}), f32[3584,128]{0,1:T(8,128)}) %all-reduce.20.cloned.1.call-update) | async-done | bytes 1835024 | tf_op jit(solution)/shard_map/psum | solution.py:36
  347.2 51.6 %all-reduce.22.cloned.1.call-done = f32[128,128]{0,1:T(8,128)} async-done(((f32[128,128]{0,1:T(8,128)}), f32[128,128]{0,1:T(8,128)}) %all-reduce.22.cloned.1.call-update) | async-done | bytes 65552 | tf_op jit(solution)/shard_map/psum | solution.py:37
  400.6 11.7 %cholesky.70 = f32[128,128]{1,0:T(8,128)S(1)} custom-call(f32[128,128]{1,0:T(8,128)S(1)} %fusion.11), custom_call_target="Cholesky" | custom-call | tf_op jit(solution)/shard_map/jit(cholesky)/cholesky | solution.py:38
  413.7 9.8 %custom-call.8 = f32[1,128,128]{1,2,0:T(8,128)S(1)} custom-call(f32[1,128,128]{2,1,0:T(8,128)S(1)} %fusion.6), custom_call_target="InvertDiagBlocksLowerTriangular" | custom-call | tf_op jit(solution)/shard_map/triangular_solve | solution.py:30
  426.5 11.0 %fusion.2 = bf16[2048,128]{0,1:T(8,128)(2,1)} fusion(bf16[3584,128]{1,0:T(8,128)(2,1)S(1)} %convolution_convert_fusion, bf16[2048,3584]{1,0:T(8,128)(2,1)} %param.7), kind=kOutput, calls=%fused_computation.8 | convolution fusion | flops 1879310336 | bytes 16121856 | tf_op jit(solution)/shard_map/dot_general | solution.py:52
  437.5 8.3 %all-reduce.26.cloned.1.call-start = ((), (), s32[]{:S(2)}) async-start(), calls=%async_computation.7 | async-start | bytes 1048576 | tf_op jit(solution)/shard_map/psum | solution.py:36
  445.9 45.8 %all-reduce.24.cloned.1.call-done = bf16[2048,128]{0,1:T(8,128)(2,1)} async-done(((bf16[2048,128]{0,1:T(8,128)(2,1)}), bf16[2048,128]{0,1:T(8,128)(2,1)}) %all-reduce.24.cloned.1.call-update) | async-done | bytes 524304 | tf_op jit(solution)/shard_map/psum | solution.py:16
  495.6 37.7 %all-reduce.26.cloned.1.call-done = f32[1024,128]{0,1:T(8,128)} async-done(((f32[1024,128]{0,1:T(8,128)}), f32[1024,128]{0,1:T(8,128)}) %all-reduce.26.cloned.1.call-update) | async-done | bytes 524304 | tf_op jit(solution)/shard_map/psum | solution.py:36
  535.8 53.9 %all-reduce.28.cloned.1.call-done = f32[128,128]{0,1:T(8,128)} async-done(((f32[128,128]{0,1:T(8,128)}), f32[128,128]{0,1:T(8,128)}) %all-reduce.28.cloned.1.call-update) | async-done | bytes 65552 | tf_op jit(solution)/shard_map/psum | solution.py:37
  591.5 11.7 %cholesky.81 = f32[128,128]{1,0:T(8,128)S(1)} custom-call(f32[128,128]{1,0:T(8,128)S(1)} %fusion.9), custom_call_target="Cholesky" | custom-call | tf_op jit(solution)/shard_map/jit(cholesky)/cholesky | solution.py:38
  604.5 9.8 %custom-call.11 = f32[1,128,128]{1,2,0:T(8,128)S(1)} custom-call(f32[1,128,128]{2,1,0:T(8,128)S(1)} %fusion.7), custom_call_target="InvertDiagBlocksLowerTriangular" | custom-call | tf_op jit(solution)/shard_map/triangular_solve/custom-call.0 | solution.py:30
  616.0 4.5 fusion.1
  620.6 54.0 %all-reduce.30.cloned.1.call-done = bf16[2048,128]{0,1:T(8,128)(2,1)} async-done(((bf16[2048,128]{0,1:T(8,128)(2,1)}), bf16[2048,128]{0,1:T(8,128)(2,1)}) %all-reduce.30.cloned.1.call-update) | async-done | bytes 524304 | tf_op jit(solution)/shard_map/psum | solution.py:16
  674.6 8.7 %fusion.21 = f32[128,3584]{1,0:T(8,128)} fusion(bf16[2048,128]{0,1:T(8,128)(2,1)} %all-reduce.30.cloned.1.call-done, bf16[2048,3584]{1,0:T(8,128)(2,1)} %param.7), kind=kOutput, calls=%fused_computation.44 | convolution fusion | flops 1879048192 | bytes 17039360 | tf_op jit(solution)/shard_map/dot_general | solution.py:10
  684.3 76.2 %all-reduce.32.cloned.1.call-done = f32[128,3584]{1,0:T(8,128)} async-done(((f32[128,3584]{1,0:T(8,128)}), f32[128,3584]{1,0:T(8,128)}) %all-reduce.32.cloned.1.call-update) | async-done | bytes 1835024 | tf_op jit(solution)/shard_map/psum | solution.py:59
  (50 shorter events, 38.6 us)
Async XLA Ops:
  7.2 1.2 copy-start
  7.2 66.7 %all-reduce.12.cloned.1.call-start = ((), (), s32[]{:S(2)}) async-start(), calls=%async_computation | async-start | bytes 1048576 | tf_op jit(solution)/shard_map/psum | solution.py:16
  16.5 99.0 %all-reduce.14.cloned.1.call-start = ((), (), s32[]{:S(2)}) async-start(), calls=%async_computation.1 | async-start | bytes 1048576 | tf_op jit(solution)/shard_map/psum | solution.py:36
  77.8 94.1 %all-reduce.16.cloned.1.call-start = ((), (), s32[]{:S(2)}) async-start(), calls=%async_computation.2 | async-start | bytes 131072 | tf_op jit(solution)/shard_map/psum | solution.py:37
  117.9 138.9 %all-reduce.18.cloned.1.call-start = ((), (), s32[]{:S(2)}) async-start(), calls=%async_computation.3 | async-start | bytes 1048576 | tf_op jit(solution)/shard_map/psum | solution.py:16
  202.8 139.9 %all-reduce.20.cloned.1.call-start = ((), (), s32[]{:S(2)}) async-start(), calls=%async_computation.4 | async-start | bytes 3670016 | tf_op jit(solution)/shard_map/psum | solution.py:36
  265.5 133.3 %all-reduce.22.cloned.1.call-start = ((), (), s32[]{:S(2)}) async-start(), calls=%async_computation.5 | async-start | bytes 131072 | tf_op jit(solution)/shard_map/psum | solution.py:37
  342.7 80.8 %copy-start.1 = (f32[3584,128]{0,1:T(8,128)S(1)}, f32[3584,128]{0,1:T(8,128)}, u32[]{:S(2)}) copy-start(f32[3584,128]{0,1:T(8,128)} %all-reduce.20.cloned.1.call-done) | copy-start | bytes 5505028
  347.2 144.5 %all-reduce.24.cloned.1.call-start = ((), (), s32[]{:S(2)}) async-start(), calls=%async_computation.6 | async-start | bytes 1048576 | tf_op jit(solution)/shard_map/psum | solution.py:16
  437.5 95.7 %all-reduce.26.cloned.1.call-start = ((), (), s32[]{:S(2)}) async-start(), calls=%async_computation.7 | async-start | bytes 1048576 | tf_op jit(solution)/shard_map/psum | solution.py:36
  495.5 94.1 %all-reduce.28.cloned.1.call-start = ((), (), s32[]{:S(2)}) async-start(), calls=%async_computation.8 | async-start | bytes 131072 | tf_op jit(solution)/shard_map/psum | solution.py:37
  535.7 138.9 %all-reduce.30.cloned.1.call-start = ((), (), s32[]{:S(2)}) async-start(), calls=%async_computation.9 | async-start | bytes 1048576 | tf_op jit(solution)/shard_map/psum | solution.py:16
  620.6 139.9 %all-reduce.32.cloned.1.call-start = ((), (), s32[]{:S(2)}) async-start(), calls=%async_computation.10 | async-start | bytes 3670016 | tf_op jit(solution)/shard_map/psum | solution.py:59
Sparse Core Ops, SparseCore 0:
  16.6 57.2 all-reduce.11
  77.9 37.5 all-reduce.13
  119.4 52.4 all-reduce.15
  202.9 53.9 all-reduce.17
  265.7 76.9 all-reduce.19
  347.3 51.5 all-reduce.21
  437.7 53.9 all-reduce.23
  495.7 37.5 all-reduce.25
  537.2 52.4 all-reduce.27
  620.7 53.9 all-reduce.29
  683.5 76.9 all-reduce.31
where the time goes:
time: 779 us; the launch traced here: 770 us
  waiting for transfers between devices  599 us (77%)
  other arithmetic  71.1 us (9%)
  matrix products  68.8 us (9%)
  between operations  14.2 us (2%)
  starting transfers between devices  8.99 us (1%)
    psum x4, waiting for transfers between devices, token_total(): return lax.psum(partial_value.astype(jnp.bfloat16), 'mp')  211 us
    psum x3, waiting for transfers between devices, orthonormalize(): gram_matrix = lax.psum(gram_of(summed), 'mp')  159 us
    psum x3, waiting for transfers between devices, orthonormalize(): summed = lax.psum(partial_value, 'dp')  152 us
    psum x1, waiting for transfers between devices, on_device(): projection = lax.psum(projected, 'dp')  76.2 us
    another operation x9, other arithmetic, orthonormalize(): factor = jnp.linalg.cholesky(gram_matrix)  37.2 us
    another operation x6, other arithmetic, solve_rows(): lax.linalg.triangular_solve(factor, matrix, left_side=False, lower=True,...  31.4 us
    dot_general x4, matrix products, contract_rows(): lax.dot_general(left, right, (((0,), (0,)), ((), ())), preferred_element_...  25.1 us
  transfers between devices with their start and end apart: 11, of which 11 were waited for; matrix products, arithmetic and copies ran while one was open for 0% of the time, Pallas kernels for 0%

commit v1 on v0

v1 whole, which is shorter than its diff:
```python
import functools

import jax
import jax.numpy as jnp
from jax import lax
from jax.experimental import pallas as pl
from jax.experimental.pallas import tpu as pltpu
from jax.sharding import PartitionSpec as P

H = 8192
F32, BF16 = jnp.float32, jnp.bfloat16
MESH = pl.DeviceIdType.MESH


def inverse_factor(gram):
    k = gram.shape[0]
    row_id = lax.broadcasted_iota(jnp.int32, (k, k), 0)
    lane_id = lax.broadcasted_iota(jnp.int32, (k, k), 1)
    row_of = lax.broadcasted_iota(jnp.int32, (k, 1), 0)
    eye = row_id == lane_id

    def step(j, carry):
        m, e = carry
        col = jnp.sum(jnp.where(lane_id == j, m, 0.0), axis=1, keepdims=True)
        row = jnp.sum(jnp.where(row_id == j, m, 0.0), axis=0, keepdims=True)
        done = jnp.sum(jnp.where(row_id == j, e, 0.0), axis=0, keepdims=True)
        pivot = jnp.sum(jnp.where(row_of == j, col, 0.0), axis=0, keepdims=True)
        scale = jnp.where(row_of > j, col * (1.0 / pivot), 0.0)
        return m - scale * row, e - scale * done

    m, e = lax.fori_loop(0, k, step, (gram, jnp.where(eye, 1.0, 0.0).astype(F32)))
    pivots = jnp.sum(jnp.where(eye, m, 0.0), axis=1, keepdims=True)
    return e * lax.rsqrt(pivots)


def kernel(
    n_dp, n_mp, acts, grads, probe, basis_t, proj,
    acts_v, grads_v, probe_v,
    part0, part1, part2, part3, came0, came1, came2, came3, rows0, rows1, rows2, rows3,
    sent0, sent1, sent2, sent3, got0, got1, got2, got3, sk0, sk1, sk2,
    gram_part, gram_came, gram_all, factor,
    load_sem, mp_send, mp_recv, dp_send, dp_recv, g_send, g_recv,
):
    me_d, me_m = lax.axis_index("dp"), lax.axis_index("mp")
    tokens, k = acts_v.shape[0], probe_v.shape[1]
    span = tokens // n_mp
    parts, cames = (part0, part1, part2, part3), (came0, came1, came2, came3)
    rows = (rows0, rows1, rows2, rows3)
    sents, gots = (sent0, sent1, sent2, sent3), (got0, got1, got2, got3)
    sketches = (sk0, sk1, sk2, proj)

    def span_of(c):
        return pl.ds(pl.multiple_of(c * span, span), span)

    def grads_load(c):
        return pltpu.make_async_copy(
            grads.at[span_of(c), :], grads_v.at[span_of(c), :], load_sem.at[c]
        )

    probe_load = pltpu.make_async_copy(probe, probe_v, load_sem.at[n_mp])
    acts_load = pltpu.make_async_copy(acts, acts_v, load_sem.at[n_mp + 1])
    probe_load.start()
    for i in range(n_mp):
        grads_load(lax.rem(me_m + 1 + i, n_mp)).start()
    acts_load.start()

    barrier = pltpu.get_barrier_semaphore()
    for i in range(1, n_mp):
        pl.semaphore_signal(
            barrier, inc=1, device_id={"mp": lax.rem(me_m + i, n_mp)}, device_id_type=MESH
        )
    for i in range(1, n_dp):
        pl.semaphore_signal(
            barrier, inc=1, device_id={"dp": lax.rem(me_d + i, n_dp)}, device_id_type=MESH
        )
    probe_load.wait()
    pl.semaphore_wait(barrier, n_mp + n_dp - 2)

    def copy(axis, src, dst, send, recv, peer):
        return pltpu.make_async_remote_copy(
            src_ref=src, dst_ref=dst, send_sem=send, recv_sem=recv,
            device_id={axis: peer}, device_id_type=MESH,
        )

    def gather_rows(s, piece):
        target = rows[s].at[:, span_of(me_m)]
        target[...] = piece.astype(BF16)

        def send(i, _):
            peer = lax.rem(me_m + i, n_mp)
            copy("mp", target, target, mp_send.at[s, 1, peer], mp_recv.at[s, 1, me_m], peer).start()
            return 0

        def wait(i, _):
            peer = lax.rem(me_m + i, n_mp)
            theirs = rows[s].at[:, span_of(peer)]
            copy("mp", target, theirs, mp_send.at[s, 1, peer], mp_recv.at[s, 1, peer], peer).wait()
            return 0

        lax.fori_loop(1, n_mp, send, 0)
        lax.fori_loop(1, n_mp, wait, 0)

    def scatter_rows(s, product, first, last):
        def body(i, _):
            c = lax.rem(me_m + i, n_mp)
            parts[s].at[c][...] = product(c).astype(BF16)

            @pl.when(i < n_mp)
            def _():
                copy(
                    "mp", parts[s].at[c], cames[s].at[me_m],
                    mp_send.at[s, 0, c], mp_recv.at[s, 0, me_m], c,
                ).start()

            return 0

        lax.fori_loop(first, last, body, 0)

    def collect_rows(s):
        def add(i, total):
            peer = lax.rem(me_m + i, n_mp)
            copy(
                "mp", parts[s].at[peer], cames[s].at[peer],
                mp_send.at[s, 0, peer], mp_recv.at[s, 0, peer], peer,
            ).wait()
            return total + cames[s].at[peer][...].astype(F32)

        return lax.fori_loop(1, n_mp, add, parts[s].at[me_m][...].astype(F32))

    def sum_tokens(s, field):
        width = field.shape[1] // n_dp

        def cols(j):
            return pl.ds(pl.multiple_of(j * width, 128), width)

        def body(i, _):
            j = lax.rem(me_d + i, n_dp)
            sents[s].at[j][...] = jnp.dot(
                rows[s][...], field[:, cols(j)], preferred_element_type=F32
            ).astype(BF16)

            @pl.when(i < n_dp)
            def _():
                copy(
                    "dp", sents[s].at[j], gots[s].at[me_d],
                    dp_send.at[s, 0, j], dp_recv.at[s, 0, me_d], j,
                ).start()

            return 0

        lax.fori_loop(1, n_dp + 1, body, 0)
        total = sents[s].at[me_d][...].astype(F32)
        for i in range(1, n_dp):
            peer = lax.rem(me_d + i, n_dp)
            copy(
                "dp", sents[s].at[peer], gots[s].at[peer],
                dp_send.at[s, 0, peer], dp_recv.at[s, 0, peer], peer,
            ).wait()
            total = total + gots[s].at[peer][...].astype(F32)
        target = sketches[s].at[:, cols(me_d)]
        target[...] = total.astype(BF16)
        for i in range(1, n_dp):
            peer = lax.rem(me_d + i, n_dp)
            copy("dp", target, target, dp_send.at[s, 1, peer], dp_recv.at[s, 1, me_d], peer).start()
        for i in range(1, n_dp):
            peer = lax.rem(me_d + i, n_dp)
            theirs = sketches[s].at[:, cols(peer)]
            copy("dp", target, theirs, dp_send.at[s, 1, peer], dp_recv.at[s, 1, peer], peer).wait()

    g_rows = k // n_mp

    def g_span(c):
        return pl.ds(pl.multiple_of(c * g_rows, g_rows), g_rows)

    def gram_start(s):
        sketch = sketches[s][...]
        gram_part.at[s][...] = lax.dot_general(
            sketch, sketch, (((1,), (1,)), ((), ())), preferred_element_type=F32
        )
        gram_came.at[s, me_m][...] = gram_part.at[s, g_span(me_m), :][...]
        for i in range(1, n_mp):
            peer = lax.rem(me_m + i, n_mp)
            copy(
                "mp", gram_part.at[s, g_span(peer), :], gram_came.at[s, me_m],
                g_send.at[s, 0, peer], g_recv.at[s, 0, me_m], peer,
            ).start()

    def gram_middle(s):
        for i in range(1, n_mp):
            peer = lax.rem(me_m + i, n_mp)
            copy(
                "mp", gram_part.at[s, g_span(peer), :], gram_came.at[s, peer],
                g_send.at[s, 0, peer], g_recv.at[s, 0, peer], peer,
            ).wait()
        target = gram_all.at[s, g_span(me_m), :]
        total = gram_came.at[s, 0][...]
        for i in range(1, n_mp):
            total = total + gram_came.at[s, i][...]
        target[...] = total
        for i in range(1, n_mp):
            peer = lax.rem(me_m + i, n_mp)
            copy("mp", target, target, g_send.at[s, 1, peer], g_recv.at[s, 1, me_m], peer).start()

    def gram_end(s):
        target = gram_all.at[s, g_span(me_m), :]
        for i in range(1, n_mp):
            peer = lax.rem(me_m + i, n_mp)
            theirs = gram_all.at[s, g_span(peer), :]
            copy("mp", target, theirs, g_send.at[s, 1, peer], g_recv.at[s, 1, peer], peer).wait()
        factor[...] = inverse_factor(gram_all.at[s][...])

    def probe_product(c):
        grads_load(c).wait()
        return jnp.dot(grads_v[span_of(c), :], probe_v[...], preferred_element_type=F32)

    scatter_rows(0, probe_product, 1, n_mp + 1)
    gather_rows(0, collect_rows(0).T)
    acts_load.wait()

    for s, (field, into) in enumerate(((acts_v, acts_v), (grads_v, grads_v), (acts_v, acts_v))):
        sum_tokens(s, field)
        gram_start(s)

        def product(c, s=s, into=into):
            return lax.dot_general(
                into[span_of(c), :], sketches[s][...],
                (((1,), (1,)), ((), ())), preferred_element_type=F32,
            )

        scatter_rows(s + 1, product, 1, n_mp // 2 + 1)
        gram_middle(s)
        scatter_rows(s + 1, product, n_mp // 2 + 1, n_mp + 1)
        gram_end(s)
        total = collect_rows(s + 1)
        gather_rows(
            s + 1,
            lax.dot_general(
                factor[...], total, (((1,), (1,)), ((), ())),
                precision=lax.Precision.HIGHEST, preferred_element_type=F32,
            ),
        )
    basis_t[...] = jnp.dot(
        factor[...], sk2[...].astype(F32),
        precision=lax.Precision.HIGHEST, preferred_element_type=F32,
    )
    sum_tokens(3, grads_v)


def fused(n_dp, n_mp, activations, output_grads, probe_matrix):
    tokens, features = activations.shape
    units, k = probe_matrix.shape
    span = tokens // n_mp
    widths = (features, units, features, units)
    any_space = pl.BlockSpec(memory_space=pl.ANY)
    vmem = pl.BlockSpec(memory_space=pltpu.VMEM)
    pieces = [pltpu.VMEM((n_mp, span, k), BF16)] * 4
    columns = [pltpu.VMEM((n_dp, k, w // n_dp), BF16) for w in widths]
    basis_t, proj = pl.pallas_call(
        functools.partial(kernel, n_dp, n_mp),
        out_shape=(
            jax.ShapeDtypeStruct((k, features), F32),
            jax.ShapeDtypeStruct((k, units), BF16),
        ),
        in_specs=[any_space] * 3,
        out_specs=(vmem, vmem),
        scratch_shapes=[
            pltpu.VMEM(activations.shape, BF16),
            pltpu.VMEM(output_grads.shape, BF16),
            pltpu.VMEM(probe_matrix.shape, BF16),
            *pieces,
            *pieces,
            *[pltpu.VMEM((k, tokens), BF16)] * 4,
            *columns,
            *columns,
            *[pltpu.VMEM((k, w), BF16) for w in widths[:3]],
            pltpu.VMEM((3, k, k), F32),
            pltpu.VMEM((3, n_mp, k // n_mp, k), F32),
            pltpu.VMEM((3, k, k), F32),
            pltpu.VMEM((k, k), F32),
            pltpu.SemaphoreType.DMA((n_mp + 2,)),
            pltpu.SemaphoreType.DMA((4, 2, n_mp)),
            pltpu.SemaphoreType.DMA((4, 2, n_mp)),
            pltpu.SemaphoreType.DMA((4, 2, n_dp)),
            pltpu.SemaphoreType.DMA((4, 2, n_dp)),
            pltpu.SemaphoreType.DMA((3, 2, n_mp)),
            pltpu.SemaphoreType.DMA((3, 2, n_mp)),
        ],
        compiler_params=pltpu.CompilerParams(
            collective_id=0, has_side_effects=True, vmem_limit_bytes=56 * 2**20
        ),
    )(activations, output_grads, probe_matrix)
    return (basis_t * jnp.sqrt(F32(H))).T, proj.astype(F32)


def contract_rows(left, right):
    return lax.dot_general(left, right, (((0,), (0,)), ((), ())), preferred_element_type=F32)


def token_total(partial_value):
    return lax.psum(partial_value.astype(BF16), "mp")


def orthonormalize(partial_value):
    summed = lax.psum(partial_value, "dp")
    gram = lax.dot_general(
        summed, summed, (((0,), (0,)), ((), ())),
        precision=lax.Precision.HIGHEST, preferred_element_type=F32,
    )
    factor = jnp.linalg.cholesky(lax.psum(gram, "mp"))
    return lax.linalg.triangular_solve(
        factor, summed, left_side=False, lower=True, transpose_a=True
    )


def separate(activations, output_grads, probe_matrix):
    def rows_of(field, columns):
        return token_total(jnp.dot(field, columns.astype(BF16), preferred_element_type=F32))

    first = orthonormalize(contract_rows(activations, rows_of(output_grads, probe_matrix)))
    second = orthonormalize(contract_rows(output_grads, rows_of(activations, first)))
    third = orthonormalize(contract_rows(activations, rows_of(output_grads, second)))
    projection = lax.psum(contract_rows(rows_of(activations, third), output_grads), "dp")
    return third * jnp.sqrt(F32(H)), projection


def solution(mesh):
    n_dp, n_mp = mesh.shape["dp"], mesh.shape["mp"]

    def on_device(activations, output_grads, probe_matrix):
        tokens, features = activations.shape
        units, k = probe_matrix.shape
        even = (
            features % (128 * n_dp) == 0
            and units % (128 * n_dp) == 0
            and tokens % (128 * n_mp) == 0
            and k % (8 * n_mp) == 0
        )
        run = functools.partial(fused, n_dp, n_mp) if even else separate
        return run(activations, output_grads, probe_matrix)

    in_specs = (P("dp", "mp"), P("dp", "mp"), P("mp", None))
    out_specs = (P("mp", None), P(None, "mp"))
    return jax.shard_map(
        on_device, mesh=mesh, in_specs=in_specs, out_specs=out_specs, check_vma=False
    )
```

time: 779 us -> 244 us (0.31)
  waiting for transfers between devices: 599 us -> 0 us
  Pallas kernels: 0 us -> 236 us
  matrix products: 68.8 us -> 0 us
  other arithmetic: 71.1 us -> 3.68 us
  between operations: 14.2 us -> 0.64 us
  starting transfers between devices: 8.99 us -> 0 us
    psum x11 -> x0, waiting for transfers between devices: 599 us -> none  [the longest x4 211 us: token_total(): return lax.psum(partial_value.astype(jnp.bfloat16), 'mp')]
    pallas_call x0 -> x1, Pallas kernels: none -> 236 us  [fused(): pl.pallas_call(functools.partial(kernel, n_dp, n_mp), out_shape=(jax.Shap...]
    another operation x15 -> x0, other arithmetic: 68.6 us -> none  [the longest x9 37.2 us: orthonormalize(): factor = jnp.linalg.cholesky(gram_matrix)]
    dot_general x11 -> x0, matrix products: 62.5 us -> none  [the longest x4 25.1 us: contract_rows(): lax.dot_general(left, right, (((0,), (0,)), ((), ())), preferred_element_...]
    psum x11 -> x0, starting transfers between devices: 8.99 us -> none  [the longest x3 8.66 us: orthonormalize(): summed = lax.psum(partial_value, 'dp')]
  transfers between devices with their start and end apart: 11 -> 0, of which waited for: 11 -> 0; matrix products, arithmetic and copies ran while one was open for 0% -> 0% of each run, Pallas kernels for 0% -> 0%
where the time goes in v1:
time: 244 us; the launch traced here: 241 us
  Pallas kernels  236 us (97%)
  other arithmetic  3.68 us (2%)
    pallas_call x1, Pallas kernels, fused(): pl.pallas_call(functools.partial(kernel, n_dp, n_mp), out_shape=(jax.Shap...  236 us

profile of v1, /device:TPU:0, one launch (start us, length us, event | category | flops | bytes accessed | tf_op | source)
XLA Modules:
  0.0 241.0 jit_solution(8554507578279260726)
XLA Ops:
  0.6 235.6 %shard_map.50 = (f32[128,1024]{1,0:T(8,128)}, bf16[128,3584]{1,0:T(8,128)(2,1)}) custom-call(bf16[2048,1024]{1,0:T(8,128)(2,1)} %acts.1, bf16[2048,3584]{1,0:T(8,128)(2,1)} %grads.1, bf16[3584,128]{1,0:T(8,128)(2,1)} %probe.1), custom_call_target="tpu_custom_call" | custom-call | tf_op jit(solution)/shard_map/pallas_call | solution.py:258
  236.3 1.1 multiply_bitcast_fusion
  237.4 1.0 copy.5
  238.4 2.6 %convert_element_type.3 = f32[128,3584]{1,0:T(8,128)} convert(bf16[128,3584]{1,0:T(8,128)(2,1)} %get-tuple-element.5) | non-fusion elementwise | flops 458752 | bytes 2752512 | tf_op jit(solution)/shard_map/convert_element_type | solution.py:292

commit v2 on v1

--- a/solution.py
+++ b/solution.py
@@ -16,19 +16,40 @@
     k = gram.shape[0]
     row_id = lax.broadcasted_iota(jnp.int32, (k, k), 0)
     lane_id = lax.broadcasted_iota(jnp.int32, (k, k), 1)
+    lane_of = lax.broadcasted_iota(jnp.int32, (8, k), 1)
     row_of = lax.broadcasted_iota(jnp.int32, (k, 1), 0)
+    group_id = lax.broadcasted_iota(jnp.int32, (k // 8, 8, k), 0)
     eye = row_id == lane_id
 
-    def step(j, carry):
+    def group_of(x, g):
+        return jnp.sum(jnp.where(group_id == g, x.reshape(k // 8, 8, k), 0.0), axis=0)
+
+    def lane_at(x, lanes, j):
+        return jnp.sum(jnp.where(lanes == j, x, 0.0), axis=1, keepdims=True)
+
+    def step(g, carry):
         m, e = carry
-        col = jnp.sum(jnp.where(lane_id == j, m, 0.0), axis=1, keepdims=True)
-        row = jnp.sum(jnp.where(row_id == j, m, 0.0), axis=0, keepdims=True)
-        done = jnp.sum(jnp.where(row_id == j, e, 0.0), axis=0, keepdims=True)
-        pivot = jnp.sum(jnp.where(row_of == j, col, 0.0), axis=0, keepdims=True)
-        scale = jnp.where(row_of > j, col * (1.0 / pivot), 0.0)
-        return m - scale * row, e - scale * done
-
-    m, e = lax.fori_loop(0, k, step, (gram, jnp.where(eye, 1.0, 0.0).astype(F32)))
+        for half in (0, 4):
+            m_rows, e_rows = group_of(m, g), group_of(e, g)
+            at = [8 * g + half + p for p in range(4)]
+            cols = [lane_at(m, lane_id, j) for j in at]
+            small = [lane_at(m_rows, lane_of, j) for j in at]
+            rows = [m_rows[half + p : half + p + 1, :] for p in range(4)]
+            done = [e_rows[half + p : half + p + 1, :] for p in range(4)]
+            for p in range(4):
+                inverse = 1.0 / small[p][half + p : half + p + 1, :]
+                for q in range(p + 1, 4):
+                    ratio = small[p][half + q : half + q + 1, :] * inverse
+                    rows[q] = rows[q] - ratio * rows[p]
+                    done[q] = done[q] - ratio * done[p]
+                    cols[q] = cols[q] - ratio * cols[p]
+                    small[q] = small[q] - ratio * small[p]
+                scale = jnp.where(row_of > at[p], cols[p] * inverse, 0.0)
+                m = m - scale * rows[p]
+                e = e - scale * done[p]
+        return m, e
+
+    m, e = lax.fori_loop(0, k // 8, step, (gram, jnp.where(eye, 1.0, 0.0).astype(F32)))
     pivots = jnp.sum(jnp.where(eye, m, 0.0), axis=1, keepdims=True)
     return e * lax.rsqrt(pivots)
 

time: 244 us -> 224 us (0.918)
  Pallas kernels: 236 us -> 216 us
    pallas_call x1, Pallas kernels: 236 us -> 216 us  [fused(): pl.pallas_call(functools.partial(kernel, n_dp, n_mp), out_shape=(jax.Shap...]
where the time goes in v2:
time: 224 us; the launch traced here: 221 us
  Pallas kernels  216 us (96%)
  other arithmetic  3.68 us (2%)
    pallas_call x1, Pallas kernels, fused(): pl.pallas_call(functools.partial(kernel, n_dp, n_mp), out_shape=(jax.Shap...  216 us

profile of v2, /device:TPU:0, one launch (start us, length us, event | category | flops | bytes accessed | tf_op | source)
XLA Modules:
  0.0 220.8 jit_solution(6026885210072706148)
XLA Ops:
  0.6 215.5 %shard_map.50 = (f32[128,1024]{1,0:T(8,128)}, bf16[128,3584]{1,0:T(8,128)(2,1)}) custom-call(bf16[2048,1024]{1,0:T(8,128)(2,1)} %acts.1, bf16[2048,3584]{1,0:T(8,128)(2,1)} %grads.1, bf16[3584,128]{1,0:T(8,128)(2,1)} %probe.1), custom_call_target="tpu_custom_call" | custom-call | tf_op jit(solution)/shard_map/pallas_call | solution.py:279
  216.1 1.1 multiply_bitcast_fusion
  217.2 1.0 copy.5
  218.2 2.6 %convert_element_type.3 = f32[128,3584]{1,0:T(8,128)} convert(bf16[128,3584]{1,0:T(8,128)(2,1)} %get-tuple-element.5) | non-fusion elementwise | flops 458752 | bytes 2752512 | tf_op jit(solution)/shard_map/convert_element_type | solution.py:313

commit v3 on v2

--- a/solution.py
+++ b/solution.py
@@ -58,16 +58,18 @@
     n_dp, n_mp, acts, grads, probe, basis_t, proj,
     acts_v, grads_v, probe_v,
     part0, part1, part2, part3, came0, came1, came2, came3, rows0, rows1, rows2, rows3,
-    sent0, sent1, sent2, sent3, got0, got1, got2, got3, sk0, sk1, sk2,
+    sent0, sent2, got0, got2, sk0, sk1, sk2,
+    up_part, up_came, cross_came, held,
     gram_part, gram_came, gram_all, factor,
     load_sem, mp_send, mp_recv, dp_send, dp_recv, g_send, g_recv,
+    out_send, in_send, up_recv, cross_recv, done_recv,
 ):
     me_d, me_m = lax.axis_index("dp"), lax.axis_index("mp")
     tokens, k = acts_v.shape[0], probe_v.shape[1]
     span = tokens // n_mp
     parts, cames = (part0, part1, part2, part3), (came0, came1, came2, came3)
     rows = (rows0, rows1, rows2, rows3)
-    sents, gots = (sent0, sent1, sent2, sent3), (got0, got1, got2, got3)
+    sents, gots = (sent0, None, sent2, None), (got0, None, got2, None)
     sketches = (sk0, sk1, sk2, proj)
 
     def span_of(c):
@@ -103,7 +105,7 @@
             device_id={axis: peer}, device_id_type=MESH,
         )
 
-    def gather_rows(s, piece):
+    def gather_rows(s, piece, meanwhile=None):
         target = rows[s].at[:, span_of(me_m)]
         target[...] = piece.astype(BF16)
 
@@ -119,6 +121,8 @@
             return 0
 
         lax.fori_loop(1, n_mp, send, 0)
+        if meanwhile is not None:
+            meanwhile()
         lax.fori_loop(1, n_mp, wait, 0)
 
     def scatter_rows(s, product, first, last):
@@ -188,6 +192,94 @@
             theirs = sketches[s].at[:, cols(peer)]
             copy("dp", target, theirs, dp_send.at[s, 1, peer], dp_recv.at[s, 1, peer], peer).wait()
 
+    def sum_tokens_line(w, s, field):
+        chunks, width = held.shape[1], held.shape[3]
+        edge = (me_d == 0) | (me_d == n_dp - 1)
+        inner = 1 + me_d // 3
+        other, outer = 3 - me_d, 3 * (me_d - 1)
+
+        def cols(half, t):
+            return pl.ds(pl.multiple_of((half * chunks + t) * width, width), width)
+
+        def product(half, t):
+            return jnp.dot(rows[s][...], field[:, cols(half, t)], preferred_element_type=F32)
+
+        def up(half, t, peer):
+            return copy(
+                "dp", up_part.at[w, half, t], up_came.at[w, half, t],
+                out_send.at[w, half, t], up_recv.at[w, half, t], peer,
+            )
+
+        def cross(half, t):
+            return copy(
+                "dp", up_part.at[w, half, t], cross_came.at[w, t],
+                in_send.at[w, 0, t], cross_recv.at[w, t], other,
+            )
+
+        def done(half, t, send, peer):
+            chunk = sketches[s].at[:, cols(half, t)]
+            return copy("dp", chunk, chunk, send, done_recv.at[w, half, t], peer)
+
+        @pl.when(edge)
+        def _():
+            def give(t, _):
+                for half in (2 - inner, inner - 1):
+                    up_part.at[w, half, t][...] = product(half, t).astype(BF16)
+                    up(half, t, inner).start()
+                return 0
+
+            def take(t, _):
+                for half in (2 - inner, inner - 1):
+                    up(half, t, inner).wait_send()
+                    done(half, t, out_send.at[w, half, t], inner).wait_recv()
+                return 0
+
+            lax.fori_loop(0, chunks, give, 0)
+            lax.fori_loop(0, chunks, take, 0)
+
+        @pl.when(jnp.logical_not(edge))
+        def _():
+            mine, theirs = me_d - 1, 2 - me_d
+
+            def body(t, _):
+                @pl.when(t < chunks)
+                def _():
+                    total = product(theirs, t)
+                    up(theirs, t, outer).wait_recv()
+                    total = total + up_came.at[w, theirs, t][...].astype(F32)
+                    up_part.at[w, theirs, t][...] = total.astype(BF16)
+                    cross(theirs, t).start()
+                    total = product(mine, t)
+                    up(mine, t, outer).wait_recv()
+                    held.at[w, t][...] = total + up_came.at[w, mine, t][...].astype(F32)
+
+                @pl.when((t >= 1) & (t < chunks + 1))
+                def _():
+                    u = t - 1
+                    cross(mine, u).wait_recv()
+                    total = held.at[w, u][...] + cross_came.at[w, u][...].astype(F32)
+                    sketches[s].at[:, cols(mine, u)][...] = total.astype(BF16)
+                    done(mine, u, out_send.at[w, 1, u], other).start()
+                    done(mine, u, out_send.at[w, 0, u], outer).start()
+
+                @pl.when(t >= 2)
+                def _():
+                    u = t - 2
+                    done(theirs, u, in_send.at[w, 1, u], other).wait_recv()
+                    done(theirs, u, in_send.at[w, 1, u], outer).start()
+
+                return 0
+
+            def end(t, _):
+                cross(theirs, t).wait_send()
+                done(mine, t, out_send.at[w, 1, t], other).wait_send()
+                done(mine, t, out_send.at[w, 0, t], outer).wait_send()
+                done(theirs, t, in_send.at[w, 1, t], outer).wait_send()
+                return 0
+
+            lax.fori_loop(0, chunks + 2, body, 0)
+            lax.fori_loop(0, chunks, end, 0)
+
     g_rows = k // n_mp
 
     def g_span(c):
@@ -238,8 +330,17 @@
     gather_rows(0, collect_rows(0).T)
     acts_load.wait()
 
+    def write_basis():
+        basis_t[...] = jnp.dot(
+            factor[...], sk2[...].astype(F32),
+            precision=lax.Precision.HIGHEST, preferred_element_type=F32,
+        )
+
     for s, (field, into) in enumerate(((acts_v, acts_v), (grads_v, grads_v), (acts_v, acts_v))):
-        sum_tokens(s, field)
+        if s == 1:
+            sum_tokens_line(0, s, field)
+        else:
+            sum_tokens(s, field)
         gram_start(s)
 
         def product(c, s=s, into=into):
@@ -259,23 +360,20 @@
                 factor[...], total, (((1,), (1,)), ((), ())),
                 precision=lax.Precision.HIGHEST, preferred_element_type=F32,
             ),
-        )
-    basis_t[...] = jnp.dot(
-        factor[...], sk2[...].astype(F32),
-        precision=lax.Precision.HIGHEST, preferred_element_type=F32,
-    )
-    sum_tokens(3, grads_v)
+            write_basis if s == 2 else None,
+        )
+    sum_tokens_line(1, 3, grads_v)
 
 
 def fused(n_dp, n_mp, activations, output_grads, probe_matrix):
     tokens, features = activations.shape
     units, k = probe_matrix.shape
     span = tokens // n_mp
-    widths = (features, units, features, units)
+    chunk, chunks = 256, units // 512
     any_space = pl.BlockSpec(memory_space=pl.ANY)
     vmem = pl.BlockSpec(memory_space=pltpu.VMEM)
     pieces = [pltpu.VMEM((n_mp, span, k), BF16)] * 4
-    columns = [pltpu.VMEM((n_dp, k, w // n_dp), BF16) for w in widths]
+    columns = [pltpu.VMEM((n_dp, k, features // n_dp), BF16)] * 2
     basis_t, proj = pl.pallas_call(
         functools.partial(kernel, n_dp, n_mp),
         out_shape=(
@@ -293,7 +391,11 @@
             *[pltpu.VMEM((k, tokens), BF16)] * 4,
             *columns,
             *columns,
-            *[pltpu.VMEM((k, w), BF16) for w in widths[:3]],
+            *[pltpu.VMEM((k, w), BF16) for w in (features, units, features)],
+            pltpu.VMEM((2, 2, chunks, k, chunk), BF16),
+            pltpu.VMEM((2, 2, chunks, k, chunk), BF16),
+            pltpu.VMEM((2, chunks, k, chunk), BF16),
+            pltpu.VMEM((2, chunks, k, chunk), F32),
             pltpu.VMEM((3, k, k), F32),
             pltpu.VMEM((3, n_mp, k // n_mp, k), F32),
             pltpu.VMEM((3, k, k), F32),
@@ -305,6 +407,11 @@
             pltpu.SemaphoreType.DMA((4, 2, n_dp)),
             pltpu.SemaphoreType.DMA((3, 2, n_mp)),
             pltpu.SemaphoreType.DMA((3, 2, n_mp)),
+            pltpu.SemaphoreType.DMA((2, 2, chunks)),
+            pltpu.SemaphoreType.DMA((2, 2, chunks)),
+            pltpu.SemaphoreType.DMA((2, 2, chunks)),
+            pltpu.SemaphoreType.DMA((2, chunks)),
+            pltpu.SemaphoreType.DMA((2, 2, chunks)),
         ],
         compiler_params=pltpu.CompilerParams(
             collective_id=0, has_side_effects=True, vmem_limit_bytes=56 * 2**20
@@ -351,8 +458,9 @@
         tokens, features = activations.shape
         units, k = probe_matrix.shape
         even = (
-            features % (128 * n_dp) == 0
-            and units % (128 * n_dp) == 0
+            n_dp == 4
+            and features % (128 * n_dp) == 0
+            and units % 512 == 0
             and tokens % (128 * n_mp) == 0
             and k % (8 * n_mp) == 0
         )

time: 224 us -> 204 us (0.911); the launches traced: 221 us -> 204 us
  Pallas kernels: 216 us -> 198 us
    pallas_call x1, Pallas kernels: 216 us -> 198 us  [fused(): pl.pallas_call(functools.partial(kernel, n_dp, n_mp), out_shape=(jax.Shap...]
where the time goes in v3:
time: 204 us
  Pallas kernels  198 us (97%)
  other arithmetic  3.68 us (2%)
    pallas_call x1, Pallas kernels, fused(): pl.pallas_call(functools.partial(kernel, n_dp, n_mp), out_shape=(jax.Shap...  198 us

profile of v3, /device:TPU:0, one launch (start us, length us, event | category | flops | bytes accessed | tf_op | source)
XLA Modules:
  0.0 203.6 jit_solution(18334334997511593597)
XLA Ops:
  0.6 198.3 %shard_map.50 = (f32[128,1024]{1,0:T(8,128)}, bf16[128,3584]{1,0:T(8,128)(2,1)}) custom-call(bf16[2048,1024]{1,0:T(8,128)(2,1)} %acts.1, bf16[2048,3584]{1,0:T(8,128)(2,1)} %grads.1, bf16[3584,128]{1,0:T(8,128)(2,1)} %probe.1), custom_call_target="tpu_custom_call" | custom-call | tf_op jit(solution)/shard_map/pallas_call | solution.py:377
  198.9 1.1 multiply_bitcast_fusion
  200.0 1.0 copy.5
  201.0 2.6 %convert_element_type.3 = f32[128,3584]{1,0:T(8,128)} convert(bf16[128,3584]{1,0:T(8,128)(2,1)} %get-tuple-element.5) | non-fusion elementwise | flops 458752 | bytes 2752512 | tf_op jit(solution)/shard_map/convert_element_type | solution.py:420

commit v4 on v3

--- a/solution.py
+++ b/solution.py
@@ -14,54 +14,64 @@
 
 def inverse_factor(gram):
     k = gram.shape[0]
-    row_id = lax.broadcasted_iota(jnp.int32, (k, k), 0)
-    lane_id = lax.broadcasted_iota(jnp.int32, (k, k), 1)
     lane_of = lax.broadcasted_iota(jnp.int32, (8, k), 1)
-    row_of = lax.broadcasted_iota(jnp.int32, (k, 1), 0)
-    group_id = lax.broadcasted_iota(jnp.int32, (k // 8, 8, k), 0)
-    eye = row_id == lane_id
-
-    def group_of(x, g):
-        return jnp.sum(jnp.where(group_id == g, x.reshape(k // 8, 8, k), 0.0), axis=0)
+    m, e = gram, jnp.where(
+        lax.broadcasted_iota(jnp.int32, (k, k), 0) == lax.broadcasted_iota(jnp.int32, (k, k), 1), 1.0, 0.0
+    ).astype(F32)
+    finished = []
+    segment = k // 4
 
     def lane_at(x, lanes, j):
         return jnp.sum(jnp.where(lanes == j, x, 0.0), axis=1, keepdims=True)
 
-    def step(g, carry):
-        m, e = carry
-        for half in (0, 4):
-            m_rows, e_rows = group_of(m, g), group_of(e, g)
-            at = [8 * g + half + p for p in range(4)]
-            cols = [lane_at(m, lane_id, j) for j in at]
-            small = [lane_at(m_rows, lane_of, j) for j in at]
-            rows = [m_rows[half + p : half + p + 1, :] for p in range(4)]
-            done = [e_rows[half + p : half + p + 1, :] for p in range(4)]
-            for p in range(4):
-                inverse = 1.0 / small[p][half + p : half + p + 1, :]
-                for q in range(p + 1, 4):
-                    ratio = small[p][half + q : half + q + 1, :] * inverse
-                    rows[q] = rows[q] - ratio * rows[p]
-                    done[q] = done[q] - ratio * done[p]
-                    cols[q] = cols[q] - ratio * cols[p]
-                    small[q] = small[q] - ratio * small[p]
-                scale = jnp.where(row_of > at[p], cols[p] * inverse, 0.0)
-                m = m - scale * rows[p]
-                e = e - scale * done[p]
-        return m, e
-
-    m, e = lax.fori_loop(0, k // 8, step, (gram, jnp.where(eye, 1.0, 0.0).astype(F32)))
-    pivots = jnp.sum(jnp.where(eye, m, 0.0), axis=1, keepdims=True)
-    return e * lax.rsqrt(pivots)
+    for first in range(0, k, segment):
+        height = k - first
+        lane_id = lax.broadcasted_iota(jnp.int32, (height, k), 1)
+        row_id = first + lax.broadcasted_iota(jnp.int32, (height, k), 0)
+        row_of = first + lax.broadcasted_iota(jnp.int32, (height, 1), 0)
+        group_id = first // 8 + lax.broadcasted_iota(jnp.int32, (height // 8, 8, k), 0)
+
+        def group_of(x, g, height=height, group_id=group_id):
+            x = x.reshape(height // 8, 8, k)
+            return jnp.sum(jnp.where(group_id == g, x, 0.0), axis=0)
+
+        def step(g, carry, lane_id=lane_id, row_of=row_of, group_of=group_of):
+            m, e = carry
+            for half in (0, 4):
+                m_rows, e_rows = group_of(m, g), group_of(e, g)
+                at = [8 * g + half + p for p in range(4)]
+                cols = [lane_at(m, lane_id, j) for j in at]
+                small = [lane_at(m_rows, lane_of, j) for j in at]
+                rows = [m_rows[half + p : half + p + 1, :] for p in range(4)]
+                done = [e_rows[half + p : half + p + 1, :] for p in range(4)]
+                for p in range(4):
+                    inverse = 1.0 / small[p][half + p : half + p + 1, :]
+                    for q in range(p + 1, 4):
+                        ratio = small[p][half + q : half + q + 1, :] * inverse
+                        rows[q] = rows[q] - ratio * rows[p]
+                        done[q] = done[q] - ratio * done[p]
+                        cols[q] = cols[q] - ratio * cols[p]
+                        small[q] = small[q] - ratio * small[p]
+                    scale = jnp.where(row_of > at[p], cols[p] * inverse, 0.0)
+                    m = m - scale * rows[p]
+                    e = e - scale * done[p]
+            return m, e
+
+        m, e = lax.fori_loop(first // 8, (first + segment) // 8, step, (m, e))
+        top = jnp.where(lane_id == row_id, m, 0.0)[:segment]
+        finished.append(e[:segment] * lax.rsqrt(jnp.sum(top, axis=1, keepdims=True)))
+        m, e = m[segment:], e[segment:]
+    return jnp.concatenate(finished, axis=0)
 
 
 def kernel(
-    n_dp, n_mp, acts, grads, probe, basis_t, proj,
+    n_dp, n_mp, acts, grads, probe, basis, proj,
     acts_v, grads_v, probe_v,
     part0, part1, part2, part3, came0, came1, came2, came3, rows0, rows1, rows2, rows3,
     sent0, sent2, got0, got2, sk0, sk1, sk2,
-    up_part, up_came, cross_came, held,
-    gram_part, gram_came, gram_all, factor,
-    load_sem, mp_send, mp_recv, dp_send, dp_recv, g_send, g_recv,
+    up_part, up_came, cross_came, row_sums,
+    gram_part, gram_came, gram_sums, gram_all, factor,
+    load_sem, mp_send, mp_recv, dp_send, dp_recv, g_send, g_recv, gd_send, gd_recv,
     out_send, in_send, up_recv, cross_recv, done_recv,
 ):
     me_d, me_m = lax.axis_index("dp"), lax.axis_index("mp")
@@ -109,21 +119,28 @@
         target = rows[s].at[:, span_of(me_m)]
         target[...] = piece.astype(BF16)
 
-        def send(i, _):
-            peer = lax.rem(me_m + i, n_mp)
-            copy("mp", target, target, mp_send.at[s, 1, peer], mp_recv.at[s, 1, me_m], peer).start()
-            return 0
-
-        def wait(i, _):
-            peer = lax.rem(me_m + i, n_mp)
+        pair = me_m + 1 - 2 * lax.rem(me_m, 2)
+        peers = [lax.rem(me_m + i, n_mp) for i in range(2, n_mp, 2)] + [pair]
+
+        def far(chunk, send, owner, peer):
+            return copy("mp", chunk, chunk, mp_send.at[s, 1, send], mp_recv.at[s, 1, owner], peer)
+
+        def twin(peer):
+            return peer + 1 - 2 * lax.rem(peer, 2)
+
+        for peer in peers:
+            far(target, peer, me_m, peer).start()
+        for peer in peers[:-1]:
             theirs = rows[s].at[:, span_of(peer)]
-            copy("mp", target, theirs, mp_send.at[s, 1, peer], mp_recv.at[s, 1, peer], peer).wait()
-            return 0
-
-        lax.fori_loop(1, n_mp, send, 0)
+            far(theirs, peer, peer, peer).wait_recv()
+            far(theirs, twin(peer), peer, pair).start()
         if meanwhile is not None:
             meanwhile()
-        lax.fori_loop(1, n_mp, wait, 0)
+        for peer in peers[:-1]:
+            theirs = rows[s].at[:, span_of(twin(peer))]
+            far(theirs, twin(peer), twin(peer), pair).wait()
+            far(target, peer, me_m, peer).wait_send()
+        far(rows[s].at[:, span_of(pair)], pair, pair, pair).wait()
 
     def scatter_rows(s, product, first, last):
         def body(i, _):
@@ -182,18 +199,23 @@
                 dp_send.at[s, 0, peer], dp_recv.at[s, 0, peer], peer,
             ).wait()
             total = total + gots[s].at[peer][...].astype(F32)
-        target = sketches[s].at[:, cols(me_d)]
-        target[...] = total.astype(BF16)
+        share = total.astype(BF16)
+        gram_part.at[s][...] = gram_of(share)
+        gram_start(s)
+        target = sketches[s].at[cols(me_d), :]
+        target[...] = total.T.astype(BF16)
         for i in range(1, n_dp):
             peer = lax.rem(me_d + i, n_dp)
             copy("dp", target, target, dp_send.at[s, 1, peer], dp_recv.at[s, 1, me_d], peer).start()
+        gram_across(s)
+        gram_middle(s)
         for i in range(1, n_dp):
             peer = lax.rem(me_d + i, n_dp)
-            theirs = sketches[s].at[:, cols(peer)]
+            theirs = sketches[s].at[cols(peer), :]
             copy("dp", target, theirs, dp_send.at[s, 1, peer], dp_recv.at[s, 1, peer], peer).wait()
 
     def sum_tokens_line(w, s, field):
-        chunks, width = held.shape[1], held.shape[3]
+        chunks, width = cross_came.shape[1], cross_came.shape[3]
         edge = (me_d == 0) | (me_d == n_dp - 1)
         inner = 1 + me_d // 3
         other, outer = 3 - me_d, 3 * (me_d - 1)
@@ -217,25 +239,58 @@
             )
 
         def done(half, t, send, peer):
-            chunk = sketches[s].at[:, cols(half, t)]
+            if s == 3:
+                chunk = sketches[s].at[:, cols(half, t)]
+            else:
+                chunk = sketches[s].at[cols(half, t), :]
             return copy("dp", chunk, chunk, send, done_recv.at[w, half, t], peer)
+
+        if s != 3:
+            gram_part.at[s][...] = jnp.zeros((k, k), F32)
+
+        def add_rows(half, t):
+            if s != 3:
+                chunk = cols(half, t)
+                row_sums[...] += jnp.dot(
+                    field[:, chunk], sketches[s][chunk, :], preferred_element_type=F32
+                )
+
+        if s != 3:
+            row_sums[...] = jnp.zeros_like(row_sums)
 
         @pl.when(edge)
         def _():
-            def give(t, _):
-                for half in (2 - inner, inner - 1):
-                    up_part.at[w, half, t][...] = product(half, t).astype(BF16)
-                    up(half, t, inner).start()
+            near, far = inner - 1, 2 - inner
+
+            def give(half, t):
+                up_part.at[w, half, t][...] = product(half, t).astype(BF16)
+                up(half, t, inner).start()
+
+            def take(half, t):
+                up(half, t, inner).wait_send()
+                done(half, t, out_send.at[w, half, t], inner).wait_recv()
+                add_rows(half, t)
+
+            def body(t, _):
+                @pl.when(t < chunks)
+                def _():
+                    give(far, t)
+
+                @pl.when((t >= 1) & (t < chunks + 1))
+                def _():
+                    give(near, t - 1)
+
+                @pl.when((t >= 3) & (t < chunks + 3))
+                def _():
+                    take(near, t - 3)
+
+                @pl.when(t >= 4)
+                def _():
+                    take(far, t - 4)
+
                 return 0
 
-            def take(t, _):
-                for half in (2 - inner, inner - 1):
-                    up(half, t, inner).wait_send()
-                    done(half, t, out_send.at[w, half, t], inner).wait_recv()
-                return 0
-
-            lax.fori_loop(0, chunks, give, 0)
-            lax.fori_loop(0, chunks, take, 0)
+            lax.fori_loop(0, chunks + 4, body, 0)
 
         @pl.when(jnp.logical_not(edge))
         def _():
@@ -249,24 +304,31 @@
                     total = total + up_came.at[w, theirs, t][...].astype(F32)
                     up_part.at[w, theirs, t][...] = total.astype(BF16)
                     cross(theirs, t).start()
-                    total = product(mine, t)
-                    up(mine, t, outer).wait_recv()
-                    held.at[w, t][...] = total + up_came.at[w, mine, t][...].astype(F32)
 
                 @pl.when((t >= 1) & (t < chunks + 1))
                 def _():
                     u = t - 1
+                    total = product(mine, u)
+                    up(mine, u, outer).wait_recv()
                     cross(mine, u).wait_recv()
-                    total = held.at[w, u][...] + cross_came.at[w, u][...].astype(F32)
-                    sketches[s].at[:, cols(mine, u)][...] = total.astype(BF16)
+                    total = total + up_came.at[w, mine, u][...].astype(F32)
+                    total = total + cross_came.at[w, u][...].astype(F32)
+                    if s == 3:
+                        sketches[s].at[:, cols(mine, u)][...] = total.astype(BF16)
+                    else:
+                        sketches[s].at[cols(mine, u), :][...] = total.T.astype(BF16)
                     done(mine, u, out_send.at[w, 1, u], other).start()
                     done(mine, u, out_send.at[w, 0, u], outer).start()
+                    if s != 3:
+                        gram_part.at[s][...] += gram_of(total.astype(BF16))
+                    add_rows(mine, u)
 
                 @pl.when(t >= 2)
                 def _():
                     u = t - 2
                     done(theirs, u, in_send.at[w, 1, u], other).wait_recv()
                     done(theirs, u, in_send.at[w, 1, u], outer).start()
+                    add_rows(theirs, u)
 
                 return 0
 
@@ -285,11 +347,12 @@
     def g_span(c):
         return pl.ds(pl.multiple_of(c * g_rows, g_rows), g_rows)
 
+    def gram_of(share):
+        return lax.dot_general(
+            share, share, (((1,), (1,)), ((), ())), preferred_element_type=F32
+        )
+
     def gram_start(s):
-        sketch = sketches[s][...]
-        gram_part.at[s][...] = lax.dot_general(
-            sketch, sketch, (((1,), (1,)), ((), ())), preferred_element_type=F32
-        )
         gram_came.at[s, me_m][...] = gram_part.at[s, g_span(me_m), :][...]
         for i in range(1, n_mp):
             peer = lax.rem(me_m + i, n_mp)
@@ -298,17 +361,31 @@
                 g_send.at[s, 0, peer], g_recv.at[s, 0, me_m], peer,
             ).start()
 
-    def gram_middle(s):
+    def gram_across(s):
         for i in range(1, n_mp):
             peer = lax.rem(me_m + i, n_mp)
             copy(
                 "mp", gram_part.at[s, g_span(peer), :], gram_came.at[s, peer],
                 g_send.at[s, 0, peer], g_recv.at[s, 0, peer], peer,
             ).wait()
-        target = gram_all.at[s, g_span(me_m), :]
         total = gram_came.at[s, 0][...]
         for i in range(1, n_mp):
             total = total + gram_came.at[s, i][...]
+        target = gram_sums.at[s, me_d]
+        target[...] = total
+        for i in range(1, n_dp):
+            peer = lax.rem(me_d + i, n_dp)
+            copy("dp", target, target, gd_send.at[s, peer], gd_recv.at[s, me_d], peer).start()
+
+    def gram_middle(s):
+        for i in range(1, n_dp):
+            peer = lax.rem(me_d + i, n_dp)
+            theirs = gram_sums.at[s, peer]
+            copy("dp", gram_sums.at[s, me_d], theirs, gd_send.at[s, peer], gd_recv.at[s, peer], peer).wait()
+        target = gram_all.at[s, g_span(me_m), :]
+        total = gram_sums.at[s, 0][...]
+        for i in range(1, n_dp):
+            total = total + gram_sums.at[s, i][...]
         target[...] = total
         for i in range(1, n_mp):
             peer = lax.rem(me_m + i, n_mp)
@@ -331,27 +408,31 @@
     acts_load.wait()
 
     def write_basis():
-        basis_t[...] = jnp.dot(
-            factor[...], sk2[...].astype(F32),
+        basis[...] = lax.dot_general(
+            sk2[...].astype(F32), factor[...], (((1,), (1,)), ((), ())),
             precision=lax.Precision.HIGHEST, preferred_element_type=F32,
         )
 
     for s, (field, into) in enumerate(((acts_v, acts_v), (grads_v, grads_v), (acts_v, acts_v))):
         if s == 1:
             sum_tokens_line(0, s, field)
+            gram_start(s)
         else:
             sum_tokens(s, field)
-        gram_start(s)
 
         def product(c, s=s, into=into):
-            return lax.dot_general(
-                into[span_of(c), :], sketches[s][...],
-                (((1,), (1,)), ((), ())), preferred_element_type=F32,
+            if s == 1:
+                return row_sums[span_of(c), :]
+            return jnp.dot(
+                into[span_of(c), :], sketches[s][...], preferred_element_type=F32
             )
 
-        scatter_rows(s + 1, product, 1, n_mp // 2 + 1)
-        gram_middle(s)
-        scatter_rows(s + 1, product, n_mp // 2 + 1, n_mp + 1)
+        if s == 1:
+            scatter_rows(s + 1, product, 1, n_mp + 1)
+            gram_across(s)
+            gram_middle(s)
+        else:
+            scatter_rows(s + 1, product, 1, n_mp + 1)
         gram_end(s)
         total = collect_rows(s + 1)
         gather_rows(
@@ -374,10 +455,10 @@
     vmem = pl.BlockSpec(memory_space=pltpu.VMEM)
     pieces = [pltpu.VMEM((n_mp, span, k), BF16)] * 4
     columns = [pltpu.VMEM((n_dp, k, features // n_dp), BF16)] * 2
-    basis_t, proj = pl.pallas_call(
+    basis, proj = pl.pallas_call(
         functools.partial(kernel, n_dp, n_mp),
         out_shape=(
-            jax.ShapeDtypeStruct((k, features), F32),
+            jax.ShapeDtypeStruct((features, k), F32),
             jax.ShapeDtypeStruct((k, units), BF16),
         ),
         in_specs=[any_space] * 3,
@@ -391,13 +472,14 @@
             *[pltpu.VMEM((k, tokens), BF16)] * 4,
             *columns,
             *columns,
-            *[pltpu.VMEM((k, w), BF16) for w in (features, units, features)],
+            *[pltpu.VMEM((w, k), BF16) for w in (features, units, features)],
             pltpu.VMEM((2, 2, chunks, k, chunk), BF16),
             pltpu.VMEM((2, 2, chunks, k, chunk), BF16),
             pltpu.VMEM((2, chunks, k, chunk), BF16),
-            pltpu.VMEM((2, chunks, k, chunk), F32),
+            pltpu.VMEM((tokens, k), F32),
             pltpu.VMEM((3, k, k), F32),
             pltpu.VMEM((3, n_mp, k // n_mp, k), F32),
+            pltpu.VMEM((3, n_dp, k // n_mp, k), F32),
             pltpu.VMEM((3, k, k), F32),
             pltpu.VMEM((k, k), F32),
             pltpu.SemaphoreType.DMA((n_mp + 2,)),
@@ -407,6 +489,8 @@
             pltpu.SemaphoreType.DMA((4, 2, n_dp)),
             pltpu.SemaphoreType.DMA((3, 2, n_mp)),
             pltpu.SemaphoreType.DMA((3, 2, n_mp)),
+            pltpu.SemaphoreType.DMA((3, n_dp)),
+            pltpu.SemaphoreType.DMA((3, n_dp)),
             pltpu.SemaphoreType.DMA((2, 2, chunks)),
             pltpu.SemaphoreType.DMA((2, 2, chunks)),
             pltpu.SemaphoreType.DMA((2, 2, chunks)),
@@ -417,7 +501,7 @@
             collective_id=0, has_side_effects=True, vmem_limit_bytes=56 * 2**20
         ),
     )(activations, output_grads, probe_matrix)
-    return (basis_t * jnp.sqrt(F32(H))).T, proj.astype(F32)
+    return basis * jnp.sqrt(F32(H)), proj.astype(F32)
 
 
 def contract_rows(left, right):
@@ -459,10 +543,12 @@
         units, k = probe_matrix.shape
         even = (
             n_dp == 4
+            and n_mp % 2 == 0
             and features % (128 * n_dp) == 0
             and units % 512 == 0
             and tokens % (128 * n_mp) == 0
             and k % (8 * n_mp) == 0
+            and k % 32 == 0
         )
         run = functools.partial(fused, n_dp, n_mp) if even else separate
         return run(activations, output_grads, probe_matrix)

time: 204 us -> 194 us (0.951)
  Pallas kernels: 198 us -> 189 us
    pallas_call x1, Pallas kernels: 198 us -> 189 us  [fused(): pl.pallas_call(functools.partial(kernel, n_dp, n_mp), out_shape=(jax.Shap...]
where the time goes in v4:
time: 194 us
  Pallas kernels  189 us (97%)
  other arithmetic  4.47 us (2%)
    pallas_call x1, Pallas kernels, fused(): pl.pallas_call(functools.partial(kernel, n_dp, n_mp), out_shape=(jax.Shap...  189 us

profile of v4, /device:TPU:0, one launch (start us, length us, event | category | flops | bytes accessed | tf_op | source)
XLA Modules:
  0.0 194.1 jit_solution(9104938873176933491)
XLA Ops:
  0.6 189.0 %shard_map.50 = (f32[1024,128]{1,0:T(8,128)}, bf16[128,3584]{1,0:T(8,128)(2,1)}) custom-call(bf16[2048,1024]{1,0:T(8,128)(2,1)} %acts.1, bf16[2048,3584]{1,0:T(8,128)(2,1)} %grads.1, bf16[3584,128]{1,0:T(8,128)(2,1)} %probe.1), custom_call_target="tpu_custom_call" | custom-call | tf_op jit(solution)/shard_map/pallas_call | solution.py:458
  189.7 1.9 broadcast_multiply_fusion
  191.5 2.6 %convert_element_type.3 = f32[128,3584]{1,0:T(8,128)} convert(bf16[128,3584]{1,0:T(8,128)(2,1)} %get-tuple-element.5) | non-fusion elementwise | flops 458752 | bytes 2752512 | tf_op jit(solution)/shard_map/convert_element_type | solution.py:504

commit v5 on v4

--- a/solution.py
+++ b/solution.py
@@ -69,7 +69,7 @@
     acts_v, grads_v, probe_v,
     part0, part1, part2, part3, came0, came1, came2, came3, rows0, rows1, rows2, rows3,
     sent0, sent2, got0, got2, sk0, sk1, sk2,
-    up_part, up_came, cross_came, row_sums,
+    up_part, up_came, cross_came,
     gram_part, gram_came, gram_sums, gram_all, factor,
     load_sem, mp_send, mp_recv, dp_send, dp_recv, g_send, g_recv, gd_send, gd_recv,
     out_send, in_send, up_recv, cross_recv, done_recv,
@@ -248,16 +248,6 @@
         if s != 3:
             gram_part.at[s][...] = jnp.zeros((k, k), F32)
 
-        def add_rows(half, t):
-            if s != 3:
-                chunk = cols(half, t)
-                row_sums[...] += jnp.dot(
-                    field[:, chunk], sketches[s][chunk, :], preferred_element_type=F32
-                )
-
-        if s != 3:
-            row_sums[...] = jnp.zeros_like(row_sums)
-
         @pl.when(edge)
         def _():
             near, far = inner - 1, 2 - inner
@@ -269,7 +259,6 @@
             def take(half, t):
                 up(half, t, inner).wait_send()
                 done(half, t, out_send.at[w, half, t], inner).wait_recv()
-                add_rows(half, t)
 
             def body(t, _):
                 @pl.when(t < chunks)
@@ -321,14 +310,12 @@
                     done(mine, u, out_send.at[w, 0, u], outer).start()
                     if s != 3:
                         gram_part.at[s][...] += gram_of(total.astype(BF16))
-                    add_rows(mine, u)
 
                 @pl.when(t >= 2)
                 def _():
                     u = t - 2
                     done(theirs, u, in_send.at[w, 1, u], other).wait_recv()
                     done(theirs, u, in_send.at[w, 1, u], outer).start()
-                    add_rows(theirs, u)
 
                 return 0
 
@@ -421,16 +408,17 @@
             sum_tokens(s, field)
 
         def product(c, s=s, into=into):
-            if s == 1:
-                return row_sums[span_of(c), :]
             return jnp.dot(
                 into[span_of(c), :], sketches[s][...], preferred_element_type=F32
             )
 
         if s == 1:
-            scatter_rows(s + 1, product, 1, n_mp + 1)
+            third = n_mp // 3 + 1
+            scatter_rows(s + 1, product, 1, third)
             gram_across(s)
+            scatter_rows(s + 1, product, third, 2 * third - 1)
             gram_middle(s)
+            scatter_rows(s + 1, product, 2 * third - 1, n_mp + 1)
         else:
             scatter_rows(s + 1, product, 1, n_mp + 1)
         gram_end(s)
@@ -476,7 +464,6 @@
             pltpu.VMEM((2, 2, chunks, k, chunk), BF16),
             pltpu.VMEM((2, 2, chunks, k, chunk), BF16),
             pltpu.VMEM((2, chunks, k, chunk), BF16),
-            pltpu.VMEM((tokens, k), F32),
             pltpu.VMEM((3, k, k), F32),
             pltpu.VMEM((3, n_mp, k // n_mp, k), F32),
             pltpu.VMEM((3, n_dp, k // n_mp, k), F32),

time: 194 us -> 193 us (level)
  no operation moved by 1% of the time
where the time goes in v5:
time: 193 us
  Pallas kernels  188 us (97%)
  other arithmetic  4.47 us (2%)
    pallas_call x1, Pallas kernels, fused(): pl.pallas_call(functools.partial(kernel, n_dp, n_mp), out_shape=(jax.Shap...  188 us

profile of v5, /device:TPU:0, one launch (start us, length us, event | category | flops | bytes accessed | tf_op | source)
XLA Modules:
  0.0 192.7 jit_solution(14859830320785481718)
XLA Ops:
  0.6 187.6 %shard_map.50 = (f32[1024,128]{1,0:T(8,128)}, bf16[128,3584]{1,0:T(8,128)(2,1)}) custom-call(bf16[2048,1024]{1,0:T(8,128)(2,1)} %acts.1, bf16[2048,3584]{1,0:T(8,128)(2,1)} %grads.1, bf16[3584,128]{1,0:T(8,128)(2,1)} %probe.1), custom_call_target="tpu_custom_call" | custom-call | tf_op jit(solution)/shard_map/pallas_call | solution.py:446
  188.2 1.9 broadcast_multiply_fusion
  190.1 2.6 %convert_element_type.3 = f32[128,3584]{1,0:T(8,128)} convert(bf16[128,3584]{1,0:T(8,128)(2,1)} %get-tuple-element.5) | non-fusion elementwise | flops 458752 | bytes 2752512 | tf_op jit(solution)/shard_map/convert_element_type | solution.py:491
